TPU v7x, 128 devices: a whole 4x4x4 slice. The times are simulated.
128 devices in a mesh: frame: 16 (over z_hi, y, core), row: 8 (over z_lo, x).
Axes of the slice: x: 4, y: 4, z: 4 (z_hi: 2, z_lo: 2; z = z_hi * 2 + z_lo), core: 2. Of those that a mesh axis runs over, the one named last changes fastest.
Arguments:
- latent: bfloat16 [16, 32, 64, 1152], P('frame', 'row'), may hold values from -1.5 to 1.5
- latent_tangent: bfloat16 [16, 32, 64, 1152], P('frame', 'row'), may hold values from -1.5 to 1.5
- modulation: float32 [3, 1152], replicated, may hold values from -3 to 3
- modulation_tangent: float32 [3, 1152], replicated, may hold values from -3 to 3
- w_qkv_s: bfloat16 [1152, 3456], replicated, may hold values from -0.1875 to 0.1875
- w_out_s: bfloat16 [1152, 1152], replicated, may hold values from -0.1875 to 0.1875
- q_gain_s: float32 [72], replicated, may hold values from 0.5 to 3
- k_gain_s: float32 [72], replicated, may hold values from 0.5 to 3
- w_qkv_t: bfloat16 [1152, 3456], replicated, may hold values from -0.1875 to 0.1875
- w_out_t: bfloat16 [1152, 1152], replicated, may hold values from -0.1875 to 0.1875
- q_gain_t: float32 [72], replicated, may hold values from 0.5 to 3
- k_gain_t: float32 [72], replicated, may hold values from 0.5 to 3
Outputs:
- output: bfloat16 [16, 32, 64, 1152], P('frame', 'row')
- output_tangent: bfloat16 [16, 32, 64, 1152], P('frame', 'row')
All inputs are finite; a program needn't handle non-finite values.
Results may differ from a plain program's by a relative error of at most 0.033.
Values may be sent and summed in bfloat16 or wider, within the bound.
A program may use at most 128 MiB of HBM per device.

v0:
```python
import functools
import math

import jax
import jax.numpy as jnp
from jax import lax
from jax.experimental import pallas as pl
from jax.experimental.pallas import tpu as pltpu
from jax.sharding import Mesh, PartitionSpec as P

D = 1152
HEADS = 16
HD = 72
EPS = 1e-06
AXES = ("zh", "y", "core", "zl", "x")
TOK = 256
HALF = 8
FACTOR = 1.0 / math.sqrt(HD)
LOG2E = 1.4426950408889634
MESH = pl.DeviceIdType.MESH
F32 = jnp.float32
BF16 = jnp.bfloat16


def coords():
    return tuple(lax.axis_index(a) for a in AXES)


def dot(a, b, dims):
    return lax.dot_general(a, b, (dims, ((), ())), preferred_element_type=F32)


def normed_hidden(count, z_of, dz_of, mod_ref, dmod_ref, put):
    rows = 32

    def step(i, _):
        at = pl.multiple_of(i * rows, rows)
        z = z_of(at, rows).astype(F32)
        dz = dz_of(at, rows).astype(F32)
        cent = z - jnp.mean(z, -1, keepdims=True)
        rstd = lax.rsqrt(jnp.mean(cent * cent, -1, keepdims=True) + EPS)
        normed = cent * rstd
        dcent = dz - jnp.mean(dz, -1, keepdims=True)
        dnormed = rstd * (dcent - normed * jnp.mean(normed * dcent, -1, keepdims=True))
        scale = 1.0 + mod_ref[1:2, :]
        hidden = normed * scale + mod_ref[0:1, :]
        dhidden = dnormed * scale + normed * dmod_ref[1:2, :] + dmod_ref[0:1, :]
        put(at, rows, hidden.astype(BF16), dhidden.astype(BF16))
        return 0

    lax.fori_loop(0, count // rows, step, 0)


def head_norm(u, du):
    r = lax.rsqrt(jnp.mean(u * u, 0, keepdims=True) + EPS)
    unit = u * r
    return unit, r * (du - unit * jnp.mean(unit * du, 0, keepdims=True))


def query_operands(q, dq, gain):
    unit, inner = head_norm(q, dq)
    qn = unit * (gain * FACTOR)
    dqn = inner * (gain * FACTOR)
    first = jnp.concatenate([qn * LOG2E, jnp.zeros_like(qn)], 0).astype(BF16)
    second = jnp.concatenate([dqn, qn], 0).astype(BF16)
    return first, second


def key_operand(k, dk, gain):
    unit, inner = head_norm(k, dk)
    both = jnp.concatenate([unit * gain, inner * gain], 0)
    return both.T.astype(BF16)


def value_operands(v, dv):
    n = v.shape[1]
    row16 = lax.broadcasted_iota(jnp.int32, (16, n), 0)
    row8 = lax.broadcasted_iota(jnp.int32, (8, n), 0)
    for_e = jnp.concatenate([v, dv, (row16 == 0).astype(F32)], 0).astype(BF16)
    for_g = jnp.concatenate([v, (row8 == 1).astype(F32)], 0).astype(BF16)
    return for_e, for_g


def normalised(acc):
    inv = 1.0 / acc[144:145]
    attn = acc[0:72] * inv
    dattn = (acc[72:144] - acc[145:146] * attn) * inv
    return attn, dattn


OFFSETS = [(a, b, d) for a in (0, 1) for b in (2, 0, 1, 3) for d in (1, 0)]
SELF = OFFSETS.index((0, 0, 0))
CHUNK = 128


def member(zh, y, zl):
    return (zh * 4 + y) * 2 + zl


def both_halves(x):
    n = x.shape[0] * 8
    return x[:, 0:8].reshape(n, D), x[:, 8:16].reshape(n, D)


def joined(z, dz):
    n = z.shape[0] // 8
    return jnp.concatenate([z.reshape(n, 8, D), dz.reshape(n, 8, D)], 1).astype(BF16)


def block_kernel(
    z_ref, dz_ref, mod_ref, dmod_ref, wqkv_s, wout_s, qg_s, kg_s, wqkv_t, wout_t, qg_t, kg_t,
    out_ref, dout_ref,
    hb, zb, stage, wtmp, wt, wos, wtt, wot, kt, qs, qd, kds, ves, vgs, acc, mx, at, mine, theirs,
    th, tx, rx, ty, got, gains,
    stage_sem, wsem, ro, rb, rz, rx_sem, ss, sw_s, sw_r, fs, fr, fl, gs, gr, gl,
):
    zh, y, c, zl, x = coords()
    right = (zh, y, c, zl, lax.rem(x + 1, 4))
    left = (zh, y, c, zl, lax.rem(x + 3, 4))
    sib = (zh, y, 1 - c, zl, x)
    partner = (zh, y, zl, c, x)
    t = lax.rem(c + zl, 2)
    me = member(zh, y, zl)
    same = t == 0
    moved = t == 1

    barrier = pltpu.get_barrier_semaphore()

    def greet(peer):
        pl.semaphore_signal(barrier, inc=1, device_id=peer, device_id_type=MESH)

    for peer in (right, left, sib):
        greet(peer)
    pl.when(moved)(lambda: greet(partner))
    for n, (a, b, d) in enumerate(OFFSETS):
        zh2, y2 = lax.rem(zh + a, 2), lax.rem(y + 4 - b, 4)
        back = (zh2, y2, zl, lax.rem(c + d, 2), x)
        if n == SELF:
            pl.when(moved)(functools.partial(greet, back))
        else:
            greet((zh2, y2, c, lax.rem(zl + d, 2), x))
            greet(back)

    out_w = [pltpu.make_async_copy(wout_s, wos, wsem.at[0]), pltpu.make_async_copy(wout_t, wot, wsem.at[1])]

    def window(j):
        cols = pl.ds(pl.multiple_of(D * j + 512 * c, 128), 640)
        return pltpu.make_async_copy(wqkv_s.at[:, cols], stage.at[j % 2], stage_sem.at[j % 2])

    def piece(i, slot):
        cols = pl.ds(pl.multiple_of(384 * i, 128), 384)
        return pltpu.make_async_copy(wqkv_t.at[:, cols], stage.at[slot, :, pl.ds(0, 384)], stage_sem.at[slot])

    window(0).start()
    window(1).start()
    for copy in out_w:
        copy.start()

    def remote(src, dst, send, recv, to):
        return pltpu.make_async_remote_copy(
            src_ref=src, dst_ref=dst, send_sem=send, recv_sem=recv, device_id=to, device_id_type=MESH
        )

    def slot(dx):
        return hb.at[2 * dx + t]

    to_right = remote(slot(0), slot(3), ss.at[0], ro.at[3], right)
    to_left = remote(slot(0), slot(1), ss.at[1], ro.at[1], left)
    to_sib = [remote(slot(dx), slot(dx), ss.at[2 + dx], rb.at[dx], sib) for dx in range(4)]
    on_left = remote(slot(1).at[0], slot(2).at[0], ss.at[6], ro.at[2], left)
    on_right = remote(slot(3).at[1], slot(2).at[1], ss.at[7], ro.at[4], right)
    swaps = [
        remote(hb.at[8, :, pl.ds(64 * q, 64)], hb.at[1, :, pl.ds(64 * q, 64)], sw_s.at[q], sw_r.at[q], partner)
        for q in range(4)
    ]
    swap_z = remote(z_ref, zb.at[0], ss.at[8], rz.at[0], partner)
    swap_dz = remote(dz_ref, zb.at[1], ss.at[9], rz.at[1], partner)

    own = 8 * t
    for q in range(4):

        def put(at_row, rows, h, dh):
            hb[own, 0, pl.ds(64 * q + at_row, rows), :] = h
            hb[own, 1, pl.ds(64 * q + at_row, rows), :] = dh

        normed_hidden(
            64,
            lambda a, n: z_ref[pl.ds(64 * q + a, n), :],
            lambda a, n: dz_ref[pl.ds(64 * q + a, n), :],
            mod_ref, dmod_ref, put,
        )
        if q == 0:
            pl.when(same)(lambda: pl.semaphore_wait(barrier, 33))
            pl.when(moved)(lambda: pl.semaphore_wait(barrier, 35))
        pl.when(moved)(swaps[q].start)

    @pl.when(same)
    def _():
        to_sib[0].start()
        to_right.start()
        to_left.start()
        zb[0] = z_ref[...]
        zb[1] = dz_ref[...]

    for j in range(3):
        window(j).wait()
        for i in range(5):
            wtmp[pl.ds(128 * i, 128), :] = stage[j % 2, :, pl.ds(128 * i, 128)].T
        if j == 0:
            window(2).start()
        else:
            piece(j - 1, j % 2).start()
        wt[pl.ds(576 * j, 576), :] = wtmp[pl.ds(pl.multiple_of(64 * c, 64), 576), :]

    for i, g in enumerate((qg_s, kg_s, qg_t, kg_t)):
        rows = lax.broadcasted_iota(jnp.int32, (HD, HD), 0)
        cols = lax.broadcasted_iota(jnp.int32, (HD, HD), 1)
        gains[i] = jnp.sum(jnp.where(rows == cols, g[...], 0.0), 1, keepdims=True)

    acc[...] = jnp.zeros_like(acc)
    mx[...] = jnp.full_like(mx, -1e30)

    def turn_piece(i, _):
        which = lax.rem(i + 1, 2)
        piece(i, which).wait()
        for n in range(3):
            rows = pl.ds(pl.multiple_of(384 * i + 128 * n, 128), 128)
            wtt[rows, :] = stage[which, :, pl.ds(128 * n, 128)].T

        @pl.when(i < 7)
        def _():
            piece(i + 2, which).start()

        return 0

    lax.fori_loop(0, 9, turn_piece, 0)

    @pl.when(moved)
    def _():
        for copy in swaps:
            copy.wait_recv()
        to_sib[0].start()
        to_right.start()
        to_left.start()
        swap_z.start()
        swap_dz.start()

    to_sib[0].wait_recv()

    for part in range(2):
        kt[0:576, 512 * part : 512 * part + 512] = dot(wt[0:576, :], hb[part].reshape(2 * TOK, D), ((1,), (1,)))

    def make_query(h, _):
        rows = pl.ds(pl.multiple_of(h * HD, 8), HD)
        for part in range(2):
            o = 512 * part
            first, second = query_operands(kt[rows, o : o + 256], kt[rows, o + 256 : o + 512], gains[0])
            qs[h, :, 256 * part : 256 * part + 256] = first
            qd[h, :, 256 * part : 256 * part + 256] = second
        return 0

    lax.fori_loop(0, HALF, make_query, 0, unroll=2)

    def two_shards(i, _):
        for n in (0, 1):

            @pl.when((i == 1 + n) & (t == n))
            def _():
                to_left.wait_recv()
                on_left.start()
                to_sib[1].start()
                to_right.wait_recv()
                on_right.start()
                to_sib[3].start()

            @pl.when((i == 1 + n) & (t != n))
            def _():
                to_sib[1].wait_recv()
                to_sib[3].wait_recv()

        @pl.when(i == 3)
        def _():
            on_left.wait_recv()
            on_right.wait_recv()
            to_sib[2].start()
            to_sib[2].wait_recv()

        first = jnp.where(i == 0, 0, i + 1)
        second = jnp.where(i == 0, 1, jnp.where(i == 3, 5, i + 5))
        for s, index in enumerate((first, second)):
            kt[:, 512 * s : 512 * s + 512] = dot(wt[576:1728, :], hb[index].reshape(2 * TOK, D), ((1,), (1,)))

        def one_head(h, _):
            krow = pl.ds(pl.multiple_of(h * HD, 8), HD)
            vrow = pl.ds(pl.multiple_of(576 + h * HD, 8), HD)
            for s in range(2):
                o = 512 * s
                keys = slice(256 * s, 256 * s + 256)
                kds[h, keys, :] = key_operand(kt[krow, o : o + 256], kt[krow, o + 256 : o + 512], gains[1])
                ve, vg = value_operands(kt[vrow, o : o + 256], kt[vrow, o + 256 : o + 512])
                ves[h, :, keys] = ve
                vgs[h, :, keys] = vg
            kd = kds[h]
            s = dot(kd, qs[h], ((1,), (0,)))
            ds = dot(kd, qd[h], ((1,), (0,)))
            old = mx[h, 0:1, :]
            new = jnp.maximum(old, jnp.max(s, 0, keepdims=True))
            mx[h, 0:1, :] = new
            e = jnp.exp2(s - new)
            g = e * ds
            keep = jnp.exp2(old - new)
            of_e = dot(ves[h], e.astype(BF16), ((1,), (0,)))
            of_g = dot(vgs[h], g.astype(BF16), ((1,), (0,)))
            acc[h, 0:72, :] = acc[h, 0:72, :] * keep + of_e[0:72]
            acc[h, 72:152, :] = acc[h, 72:152, :] * keep + of_e[72:152] + of_g
            return 0

        lax.fori_loop(0, HALF, one_head, 0, unroll=8)
        return 0

    lax.fori_loop(0, 4, two_shards, 0)

    def finish_head(h, _):
        attn, dattn = normalised(acc[h])
        rows = pl.ds(pl.multiple_of(h * HD, 8), HD)
        for part in range(2):
            for q in range(2):
                cols = slice(256 * part + 128 * q, 256 * part + 128 * q + 128)
                at[part, q, rows, 0:128] = attn[:, cols]
                at[part, q, rows, 128:256] = dattn[:, cols]
        return 0

    lax.fori_loop(0, HALF, finish_head, 0, unroll=2)
    mine[1] = at[1 - t].astype(BF16)
    trade = remote(mine.at[1], theirs, ss.at[10], rx_sem.at[0], sib)
    trade.start()
    mine[0] = at[t].astype(BF16)
    out_w[0].wait()
    out_w[1].wait()

    @pl.when(moved)
    def _():
        swap_z.wait_recv()
        swap_dz.wait_recv()

    trade.wait_recv()

    def forward(q, n):
        a, b, d = OFFSETS[n]
        to = (lax.rem(zh + a, 2), lax.rem(y + b, 4), c, lax.rem(zl + d, 2), x)
        return remote(
            tx.at[q, member(to[0], to[1], to[3])], rx.at[q, me], fs.at[16 * q + n], fr.at[16 * q + n], to
        )

    def forward_own(q):
        return pltpu.make_async_copy(tx.at[q, me], rx.at[q, me], fl.at[q])

    def give_back(q, n):
        a, b, d = OFFSETS[n]
        z2, y2, l2 = lax.rem(zh + a, 2), lax.rem(y + b, 4), lax.rem(zl + d, 2)
        return remote(
            ty.at[q, member(z2, y2, l2)], got.at[q, me], gs.at[16 * q + n], gr.at[16 * q + n], (z2, y2, l2, c, x)
        )

    def give_own(q):
        return pltpu.make_async_copy(ty.at[q, me], got.at[q, me], gl.at[q])

    others = [n for n in range(16) if n != SELF]
    gate = mod_ref[2:3, :]
    dgate = dmod_ref[2:3, :]
    lo = pl.ds(pl.multiple_of(576 * c, 16), 576)
    hi = pl.ds(pl.multiple_of(576 * (1 - c), 16), 576)

    def spatial_out(q, _):
        both = dot(mine[0, q], wos[lo, :], ((0,), (0,))) + dot(theirs[q], wos[hi, :], ((0,), (0,)))
        rows = pl.ds(pl.multiple_of(CHUNK * q, CHUNK), CHUNK)
        proj, dproj = both[0:CHUNK], both[CHUNK:]
        tx[q] = joined(
            zb[0, rows, :].astype(F32) + gate * proj,
            zb[1, rows, :].astype(F32) + gate * dproj + dgate * proj,
        )
        forward_own(q).start()
        for n in others:
            forward(q, n).start()
        return 0

    lax.fori_loop(0, 2, spatial_out, 0)

    ki = lax.broadcasted_iota(jnp.int32, (CHUNK, CHUNK), 0)
    qi = lax.broadcasted_iota(jnp.int32, (CHUNK, CHUNK), 1)
    place = (ki & 7) == (qi & 7)

    def temporal_chunk(q, _):
        forward_own(q).wait()
        for n in others:
            forward(q, n).wait_recv()

        def put(at_row, rows, h, dh):
            th[pl.ds(at_row, rows), :] = h
            th[pl.ds(CHUNK + at_row, rows), :] = dh

        def half(which):
            return lambda a, n: both_halves(rx[q, pl.ds(a // 8, n // 8)].astype(F32))[which]

        normed_hidden(CHUNK, half(0), half(1), mod_ref, dmod_ref, put)
        for j in range(3):
            kt[:, 256 * j : 256 * j + 256] = dot(wtt[D * j : D * j + D, :], th[...], ((1,), (1,)))

        def one_head(h, _):
            rows = pl.ds(pl.multiple_of(h * HD, 8), HD)
            first, second = query_operands(kt[rows, 0:128], kt[rows, 128:256], gains[2])
            kd = key_operand(kt[rows, 256:384], kt[rows, 384:512], gains[3])
            ve, vg = value_operands(kt[rows, 512:640], kt[rows, 640:768])
            both = dot(kd, jnp.concatenate([first, second], 1), ((1,), (0,)))
            s = jnp.where(place, both[:, 0:128], -1e30)
            e = jnp.exp2(s - jnp.max(s, 0, keepdims=True))
            g = e * both[:, 128:256]
            of_e = dot(ve, e.astype(BF16), ((1,), (0,)))
            of_g = dot(vg, g.astype(BF16), ((1,), (0,)))
            inv = 1.0 / of_e[144:145]
            attn = of_e[0:72] * inv
            dattn = (of_e[72:144] + of_g[0:72] - of_g[73:74] * attn) * inv
            to_rows = pl.ds(pl.multiple_of(lax.rem(h, 8) * HD, 8), HD)
            at[0, h // 8, to_rows, 0:128] = attn
            at[0, h // 8, to_rows, 128:256] = dattn
            return 0

        lax.fori_loop(0, HEADS, one_head, 0, unroll=4)
        both = dot(at[0, 0].astype(BF16), wot[0:576, :], ((0,), (0,)))
        both += dot(at[0, 1].astype(BF16), wot[576:1152, :], ((0,), (0,)))
        proj, dproj = both[0:CHUNK], both[CHUNK:]
        z, dz = both_halves(rx[q].astype(F32))
        ty[q] = joined(z + gate * proj, dz + gate * dproj + dgate * proj)
        pl.when(same)(lambda: give_own(q).start())
        pl.when(moved)(lambda: give_back(q, SELF).start())
        for n in others:
            give_back(q, n).start()
        return 0

    lax.fori_loop(0, 2, temporal_chunk, 0)

    def collect(q, _):
        pl.when(same)(lambda: give_own(q).wait())
        pl.when(moved)(lambda: give_back(q, SELF).wait())
        for n in others:
            give_back(q, n).wait()
            forward(q, n).wait_send()
        rows = pl.ds(pl.multiple_of(CHUNK * q, CHUNK), CHUNK)
        z, dz = both_halves(got[q].astype(F32))
        out_ref[rows, :] = z.astype(BF16)
        dout_ref[rows, :] = dz.astype(BF16)
        return 0

    lax.fori_loop(0, 2, collect, 0)

    for copy in (to_right, to_left, *to_sib, on_left, on_right, trade):
        copy.wait_send()

    @pl.when(moved)
    def _():
        for copy in (*swaps, swap_z, swap_dz):
            copy.wait_send()


def body(
    latent,
    latent_tangent,
    modulation,
    modulation_tangent,
    w_qkv_s,
    w_out_s,
    q_gain_s,
    k_gain_s,
    w_qkv_t,
    w_out_t,
    q_gain_t,
    k_gain_t,
):
    shape = latent.shape
    vmem = pl.BlockSpec(memory_space=pltpu.VMEM)
    hbm = pl.BlockSpec(memory_space=pl.ANY)
    dma = pltpu.SemaphoreType.DMA
    one = jax.ShapeDtypeStruct((TOK, D), BF16)
    row = lambda gain: gain.reshape(1, HD)
    out, dout = pl.pallas_call(
        block_kernel,
        out_shape=(one, one),
        in_specs=[vmem, vmem, vmem, vmem, hbm, hbm, vmem, vmem, hbm, hbm, vmem, vmem],
        out_specs=(vmem, vmem),
        scratch_shapes=[
            pltpu.VMEM((9, 2, TOK, D), BF16),
            pltpu.VMEM((2, TOK, D), BF16),
            pltpu.VMEM((2, D, 640), BF16),
            pltpu.VMEM((640, D), BF16),
            pltpu.VMEM((1728, D), BF16),
            pltpu.VMEM((D, D), BF16),
            pltpu.VMEM((3 * D, D), BF16),
            pltpu.VMEM((D, D), BF16),
            pltpu.VMEM((D, 4 * TOK), F32),
            pltpu.VMEM((HALF, 144, 2 * TOK), BF16),
            pltpu.VMEM((HALF, 144, 2 * TOK), BF16),
            pltpu.VMEM((HALF, 2 * TOK, 144), BF16),
            pltpu.VMEM((HALF, 160, 2 * TOK), BF16),
            pltpu.VMEM((HALF, 80, 2 * TOK), BF16),
            pltpu.VMEM((HALF, 160, 2 * TOK), F32),
            pltpu.VMEM((HALF, 8, 2 * TOK), F32),
            pltpu.VMEM((2, 2, 576, TOK), F32),
            pltpu.VMEM((2, 2, 576, TOK), BF16),
            pltpu.VMEM((2, 576, TOK), BF16),
            pltpu.VMEM((TOK, D), BF16),
            pltpu.VMEM((2, 16, 16, D), BF16),
            pltpu.VMEM((2, 16, 16, D), BF16),
            pltpu.VMEM((2, 16, 16, D), BF16),
            pltpu.VMEM((2, 16, 16, D), BF16),
            pltpu.VMEM((4, HD, 1), F32),
            dma((2,)), dma((2,)), dma((5,)), dma((4,)), dma((2,)), dma((1,)), dma((11,)),
            dma((4,)), dma((4,)),
            dma((32,)), dma((32,)), dma((2,)), dma((32,)), dma((32,)), dma((2,)),
        ],
        compiler_params=pltpu.CompilerParams(
            collective_id=1, has_side_effects=True, vmem_limit_bytes=63 * 2**20
        ),
        cost_estimate=pl.CostEstimate(flops=53_000_000_000, bytes_accessed=25_000_000, transcendentals=9_000_000),
        name="blocks",
    )(
        latent.reshape(TOK, D), latent_tangent.reshape(TOK, D), modulation, modulation_tangent,
        w_qkv_s, w_out_s, row(q_gain_s), row(k_gain_s), w_qkv_t, w_out_t, row(q_gain_t), row(k_gain_t),
    )
    return out.reshape(shape), dout.reshape(shape)


def solution(mesh):
    split = Mesh(mesh.devices.reshape(2, 4, 2, 2, 4), AXES)
    tokens = P(("zh", "y", "core"), ("zl", "x"), None, None)
    return jax.shard_map(
        body, mesh=split, in_specs=(tokens, tokens) + (P(),) * 10, out_specs=(tokens, tokens), check_vma=False
    )
```

profile of v0, /device:TPU:1, one launch (start us, length us, event | category | flops | bytes accessed | tf_op | source)
XLA Modules:
  0.0 122.7 jit_solution(17368587818498131771)
XLA Ops:
  0.6 118.2 %blocks.1 = (bf16[256,1152]{1,0:T(8,128)(2,1)}, bf16[256,1152]{1,0:T(8,128)(2,1)}) custom-call(bf16[256,1152]{1,0:T(8,128)(2,1)} %bitcast.10, bf16[256,1152]{1,0:T(8,128)(2,1)} %bitcast.11, f32[3,1152]{1,0:T(4,128)} %mod_ref.1, f32[3,1152]{1,0:T(4,128)} %dmod_ref.1, bf16[1152,3456]{1,0:T(8,128)(2,1)} %wqkv_s.1, bf16[1152,1152]{1,0:T(8,128)(2,1)} %wout_s.1, ...), custom_call_target="tpu_custom_call" | custom-call | flops 52999999488 | bytes 25000000 | tf_op jit(solution)/shard_map/blocks/pallas_call | solution.py:485
  118.9 1.9 %copy.16 = bf16[1,4,64,1152]{3,2,1,0:T(8,128)(2,1)} copy(bf16[1,4,64,1152]{3,2,1,0:T(8,128)(2,1)} %bitcast.9) | data formatting | bytes 1179648
  120.8 1.9 %copy.17 = bf16[1,4,64,1152]{3,2,1,0:T(8,128)(2,1)} copy(bf16[1,4,64,1152]{3,2,1,0:T(8,128)(2,1)} %bitcast.8) | data formatting | bytes 1179648
where the time goes:
time: 123 us
  Pallas kernels  118 us (96%)
  local copies, waits for them, and re-layouts  3.85 us (3%)
    pallas_call x1, Pallas kernels, body(): pl.pallas_call(block_kernel, out_shape=(one, one), in_specs=[vmem, vmem,...  118 us
    unnamed x2, local copies, waits for them, and re-layouts  3.85 us

commit v1 on v0

--- a/solution.py
+++ b/solution.py
@@ -109,10 +109,10 @@
 
 def block_kernel(
     z_ref, dz_ref, mod_ref, dmod_ref, wqkv_s, wout_s, qg_s, kg_s, wqkv_t, wout_t, qg_t, kg_t,
-    out_ref, dout_ref,
+    out_ref,
     hb, zb, stage, wtmp, wt, wos, wtt, wot, kt, qs, qd, kds, ves, vgs, acc, mx, at, mine, theirs,
     th, tx, rx, ty, got, gains,
-    stage_sem, wsem, ro, rb, rz, rx_sem, ss, sw_s, sw_r, fs, fr, fl, gs, gr, gl,
+    relay, stage_sem, wsem, ro, rb, rz, rx_sem, ss, sw_s, sw_r, fs, fr, fl, gs, gr, gl,
 ):
     zh, y, c, zl, x = coords()
     right = (zh, y, c, zl, lax.rem(x + 1, 4))
@@ -129,17 +129,23 @@
     def greet(peer):
         pl.semaphore_signal(barrier, inc=1, device_id=peer, device_id_type=MESH)
 
-    for peer in (right, left, sib):
+    z = 2 * zh + zl
+
+    def at_z(n):
+        zz = lax.rem(z + n, 4)
+        return (zz // 2, y, c, lax.rem(zz, 2), x)
+
+    plane = [(zh, lax.rem(y + n, 4), c, zl, x) for n in (1, 3)] + [at_z(1), at_z(3)]
+    for peer in (right, left, sib, *plane):
         greet(peer)
     pl.when(moved)(lambda: greet(partner))
-    for n, (a, b, d) in enumerate(OFFSETS):
-        zh2, y2 = lax.rem(zh + a, 2), lax.rem(y + 4 - b, 4)
-        back = (zh2, y2, zl, lax.rem(c + d, 2), x)
-        if n == SELF:
-            pl.when(moved)(functools.partial(greet, back))
-        else:
-            greet((zh2, y2, c, lax.rem(zl + d, 2), x))
-            greet(back)
+
+    def tell(n):
+        for peer in plane:
+            pl.semaphore_signal(relay.at[n], inc=1, device_id=peer, device_id_type=MESH)
+
+    def hear(n):
+        pl.semaphore_wait(relay.at[n], 4)
 
     out_w = [pltpu.make_async_copy(wout_s, wos, wsem.at[0]), pltpu.make_async_copy(wout_t, wot, wsem.at[1])]
 
@@ -190,8 +196,8 @@
             mod_ref, dmod_ref, put,
         )
         if q == 0:
-            pl.when(same)(lambda: pl.semaphore_wait(barrier, 33))
-            pl.when(moved)(lambda: pl.semaphore_wait(barrier, 35))
+            pl.when(same)(lambda: pl.semaphore_wait(barrier, 7))
+            pl.when(moved)(lambda: pl.semaphore_wait(barrier, 8))
         pl.when(moved)(swaps[q].start)
 
     @pl.when(same)
@@ -201,6 +207,8 @@
         to_left.start()
         zb[0] = z_ref[...]
         zb[1] = dz_ref[...]
+
+    tell(0)
 
     for j in range(3):
         window(j).wait()
@@ -212,6 +220,9 @@
             piece(j - 1, j % 2).start()
         wt[pl.ds(576 * j, 576), :] = wtmp[pl.ds(pl.multiple_of(64 * c, 64), 576), :]
 
+    hear(0)
+    tell(1)
+
     for i, g in enumerate((qg_s, kg_s, qg_t, kg_t)):
         rows = lax.broadcasted_iota(jnp.int32, (HD, HD), 0)
         cols = lax.broadcasted_iota(jnp.int32, (HD, HD), 1)
@@ -234,6 +245,23 @@
         return 0
 
     lax.fori_loop(0, 9, turn_piece, 0)
+    hear(1)
+    tell(2)
+
+    def query_rows(part):
+        kt[0:576, 0:512] = dot(wt[0:576, :], hb[part].reshape(2 * TOK, D), ((1,), (1,)))
+
+        def make_query(h, _):
+            rows = pl.ds(pl.multiple_of(h * HD, 8), HD)
+            first, second = query_operands(kt[rows, 0:256], kt[rows, 256:512], gains[0])
+            qs[h, :, 256 * part : 256 * part + 256] = first
+            qd[h, :, 256 * part : 256 * part + 256] = second
+            return 0
+
+        lax.fori_loop(0, HALF, make_query, 0, unroll=4)
+
+    pl.when(moved)(to_sib[0].wait_recv)
+    query_rows(0)
 
     @pl.when(moved)
     def _():
@@ -245,38 +273,39 @@
         swap_z.start()
         swap_dz.start()
 
-    to_sib[0].wait_recv()
-
-    for part in range(2):
-        kt[0:576, 512 * part : 512 * part + 512] = dot(wt[0:576, :], hb[part].reshape(2 * TOK, D), ((1,), (1,)))
-
-    def make_query(h, _):
-        rows = pl.ds(pl.multiple_of(h * HD, 8), HD)
-        for part in range(2):
-            o = 512 * part
-            first, second = query_operands(kt[rows, o : o + 256], kt[rows, o + 256 : o + 512], gains[0])
-            qs[h, :, 256 * part : 256 * part + 256] = first
-            qd[h, :, 256 * part : 256 * part + 256] = second
-        return 0
-
-    lax.fori_loop(0, HALF, make_query, 0, unroll=2)
+    @pl.when(same)
+    def _():
+        to_left.wait_recv()
+        on_left.start()
+        to_sib[1].start()
+        to_right.wait_recv()
+        on_right.start()
+        to_sib[3].start()
+        to_sib[0].wait_recv()
+
+    query_rows(1)
+    hear(2)
+    pl.semaphore_signal(relay.at[3], inc=1, device_id=sib, device_id_type=MESH)
 
     def two_shards(i, _):
-        for n in (0, 1):
-
-            @pl.when((i == 1 + n) & (t == n))
-            def _():
-                to_left.wait_recv()
-                on_left.start()
-                to_sib[1].start()
-                to_right.wait_recv()
-                on_right.start()
-                to_sib[3].start()
-
-            @pl.when((i == 1 + n) & (t != n))
-            def _():
-                to_sib[1].wait_recv()
-                to_sib[3].wait_recv()
+        @pl.when((i == 1) & moved)
+        def _():
+            to_sib[1].wait_recv()
+            to_sib[3].wait_recv()
+
+        @pl.when((i == 2) & moved)
+        def _():
+            to_left.wait_recv()
+            on_left.start()
+            to_sib[1].start()
+            to_right.wait_recv()
+            on_right.start()
+            to_sib[3].start()
+
+        @pl.when((i == 2) & same)
+        def _():
+            to_sib[1].wait_recv()
+            to_sib[3].wait_recv()
 
         @pl.when(i == 3)
         def _():
@@ -344,6 +373,7 @@
         swap_dz.wait_recv()
 
     trade.wait_recv()
+    pl.semaphore_wait(relay.at[3], 1)
 
     def forward(q, n):
         a, b, d = OFFSETS[n]
@@ -379,12 +409,16 @@
             zb[0, rows, :].astype(F32) + gate * proj,
             zb[1, rows, :].astype(F32) + gate * dproj + dgate * proj,
         )
+        return 0
+
+    def send(q):
         forward_own(q).start()
         for n in others:
             forward(q, n).start()
-        return 0
-
-    lax.fori_loop(0, 2, spatial_out, 0)
+
+    spatial_out(0, 0)
+    send(0)
+    spatial_out(1, 0)
 
     ki = lax.broadcasted_iota(jnp.int32, (CHUNK, CHUNK), 0)
     qi = lax.broadcasted_iota(jnp.int32, (CHUNK, CHUNK), 1)
@@ -394,6 +428,7 @@
         forward_own(q).wait()
         for n in others:
             forward(q, n).wait_recv()
+        pl.when(q == 0)(lambda: send(1))
 
         def put(at_row, rows, h, dh):
             th[pl.ds(at_row, rows), :] = h
@@ -447,8 +482,8 @@
             forward(q, n).wait_send()
         rows = pl.ds(pl.multiple_of(CHUNK * q, CHUNK), CHUNK)
         z, dz = both_halves(got[q].astype(F32))
-        out_ref[rows, :] = z.astype(BF16)
-        dout_ref[rows, :] = dz.astype(BF16)
+        out_ref[0, rows, :] = z.astype(BF16)
+        out_ref[1, rows, :] = dz.astype(BF16)
         return 0
 
     lax.fori_loop(0, 2, collect, 0)
@@ -460,6 +495,11 @@
     def _():
         for copy in (*swaps, swap_z, swap_dz):
             copy.wait_send()
+
+
+def split_kernel(both_ref, out_ref, dout_ref):
+    out_ref[...] = both_ref[0]
+    dout_ref[...] = both_ref[1]
 
 
 def body(
@@ -482,11 +522,11 @@
     dma = pltpu.SemaphoreType.DMA
     one = jax.ShapeDtypeStruct((TOK, D), BF16)
     row = lambda gain: gain.reshape(1, HD)
-    out, dout = pl.pallas_call(
+    both = pl.pallas_call(
         block_kernel,
-        out_shape=(one, one),
+        out_shape=jax.ShapeDtypeStruct((2, TOK, D), BF16),
         in_specs=[vmem, vmem, vmem, vmem, hbm, hbm, vmem, vmem, hbm, hbm, vmem, vmem],
-        out_specs=(vmem, vmem),
+        out_specs=vmem,
         scratch_shapes=[
             pltpu.VMEM((9, 2, TOK, D), BF16),
             pltpu.VMEM((2, TOK, D), BF16),
@@ -513,6 +553,7 @@
             pltpu.VMEM((2, 16, 16, D), BF16),
             pltpu.VMEM((2, 16, 16, D), BF16),
             pltpu.VMEM((4, HD, 1), F32),
+            pltpu.SemaphoreType.REGULAR((4,)),
             dma((2,)), dma((2,)), dma((5,)), dma((4,)), dma((2,)), dma((1,)), dma((11,)),
             dma((4,)), dma((4,)),
             dma((32,)), dma((32,)), dma((2,)), dma((32,)), dma((32,)), dma((2,)),
@@ -526,6 +567,13 @@
         latent.reshape(TOK, D), latent_tangent.reshape(TOK, D), modulation, modulation_tangent,
         w_qkv_s, w_out_s, row(q_gain_s), row(k_gain_s), w_qkv_t, w_out_t, row(q_gain_t), row(k_gain_t),
     )
+    out, dout = pl.pallas_call(
+        split_kernel,
+        out_shape=(one, one),
+        in_specs=[vmem],
+        out_specs=(vmem, vmem),
+        name="results",
+    )(both)
     return out.reshape(shape), dout.reshape(shape)
 
 

time: 123 us -> 116 us (0.943)
  local copies, waits for them, and re-layouts: 3.85 us -> 0 us
  Pallas kernels: 118 us -> 115 us
    unnamed x2 -> x0, local copies, waits for them, and re-layouts: 3.85 us -> none
    pallas_call x1 -> x2, Pallas kernels: 118 us -> 115 us  [the longest x1 113 us: body(): pl.pallas_call(block_kernel, out_shape=jax.ShapeDtypeStruct((2, TOK, D),...]
where the time goes in v1:
time: 116 us
  Pallas kernels  115 us (99%)
    pallas_call x1, Pallas kernels, body(): pl.pallas_call(block_kernel, out_shape=jax.ShapeDtypeStruct((2, TOK, D),...  113 us
    pallas_call x1, Pallas kernels, body(): pl.pallas_call(split_kernel, out_shape=(one, one), in_specs=[vmem], out_s...  2.32 us

profile of v1, /device:TPU:1, one launch (start us, length us, event | category | flops | bytes accessed | tf_op | source)
XLA Modules:
  0.0 115.8 jit_solution(3351627896075121813)
XLA Ops:
  0.6 112.8 %blocks.1.both_ref = bf16[2,256,1152]{2,1,0:T(8,128)(2,1)} custom-call(bf16[256,1152]{1,0:T(8,128)(2,1)} %bitcast.8, bf16[256,1152]{1,0:T(8,128)(2,1)} %bitcast.9, f32[3,1152]{1,0:T(4,128)} %mod_ref.1, f32[3,1152]{1,0:T(4,128)} %dmod_ref.1, bf16[1152,3456]{1,0:T(8,128)(2,1)} %wqkv_s.1, bf16[1152,1152]{1,0:T(8,128)(2,1)} %wout_s.1, f32[1,72]{1,0:T(1,128)} %bitcast.12, ...), custom_call_target="tpu_custom_call" | custom-call | flops 52999999488 | bytes 25000000 | tf_op jit(solution)/shard_map/blocks/pallas_call | solution.py:525
  113.5 2.3 %results.1 = (bf16[256,1152]{1,0:T(8,128)(2,1)}, bf16[256,1152]{1,0:T(8,128)(2,1)}) custom-call(bf16[2,256,1152]{2,1,0:T(8,128)(2,1)} %blocks.1.both_ref), custom_call_target="tpu_custom_call" | custom-call | tf_op jit(solution)/shard_map/results/pallas_call | solution.py:570

commit v2 on v1

--- a/solution.py
+++ b/solution.py
@@ -88,7 +88,10 @@
     return attn, dattn
 
 
-OFFSETS = [(a, b, d) for a in (0, 1) for b in (2, 0, 1, 3) for d in (1, 0)]
+OFFSETS = sorted(
+    ((a, b, d) for a in (0, 1) for b in (2, 0, 1, 3) for d in (1, 0)),
+    key=lambda o: -((1 if o[2] else 2 * o[0]) + min(o[1], 4 - o[1])),
+)
 SELF = OFFSETS.index((0, 0, 0))
 CHUNK = 128
 
@@ -109,9 +112,9 @@
 
 def block_kernel(
     z_ref, dz_ref, mod_ref, dmod_ref, wqkv_s, wout_s, qg_s, kg_s, wqkv_t, wout_t, qg_t, kg_t,
-    out_ref,
+    got,
     hb, zb, stage, wtmp, wt, wos, wtt, wot, kt, qs, qd, kds, ves, vgs, acc, mx, at, mine, theirs,
-    th, tx, rx, ty, got, gains,
+    th, tx, rx, ty, gains,
     relay, stage_sem, wsem, ro, rb, rz, rx_sem, ss, sw_s, sw_r, fs, fr, fl, gs, gr, gl,
 ):
     zh, y, c, zl, x = coords()
@@ -304,14 +307,20 @@
 
         @pl.when((i == 2) & same)
         def _():
+            on_left.wait_recv()
+            on_right.wait_recv()
+            to_sib[2].start()
             to_sib[1].wait_recv()
             to_sib[3].wait_recv()
 
-        @pl.when(i == 3)
+        @pl.when((i == 3) & moved)
         def _():
             on_left.wait_recv()
             on_right.wait_recv()
             to_sib[2].start()
+
+        @pl.when(i == 3)
+        def _():
             to_sib[2].wait_recv()
 
         first = jnp.where(i == 0, 0, i + 1)
@@ -366,6 +375,13 @@
     mine[0] = at[t].astype(BF16)
     out_w[0].wait()
     out_w[1].wait()
+    lo = pl.ds(pl.multiple_of(576 * c, 16), 576)
+    hi = pl.ds(pl.multiple_of(576 * (1 - c), 16), 576)
+
+    def own_heads(q):
+        return dot(mine[0, q], wos[lo, :], ((0,), (0,)))
+
+    own_part = own_heads(0)
 
     @pl.when(moved)
     def _():
@@ -398,27 +414,24 @@
     others = [n for n in range(16) if n != SELF]
     gate = mod_ref[2:3, :]
     dgate = dmod_ref[2:3, :]
-    lo = pl.ds(pl.multiple_of(576 * c, 16), 576)
-    hi = pl.ds(pl.multiple_of(576 * (1 - c), 16), 576)
-
-    def spatial_out(q, _):
-        both = dot(mine[0, q], wos[lo, :], ((0,), (0,))) + dot(theirs[q], wos[hi, :], ((0,), (0,)))
-        rows = pl.ds(pl.multiple_of(CHUNK * q, CHUNK), CHUNK)
+
+    def spatial_out(q, part):
+        both = part + dot(theirs[q], wos[hi, :], ((0,), (0,)))
+        rows = pl.ds(CHUNK * q, CHUNK)
         proj, dproj = both[0:CHUNK], both[CHUNK:]
         tx[q] = joined(
             zb[0, rows, :].astype(F32) + gate * proj,
             zb[1, rows, :].astype(F32) + gate * dproj + dgate * proj,
         )
-        return 0
 
     def send(q):
         forward_own(q).start()
         for n in others:
             forward(q, n).start()
 
-    spatial_out(0, 0)
+    spatial_out(0, own_part)
     send(0)
-    spatial_out(1, 0)
+    spatial_out(1, own_heads(1))
 
     ki = lax.broadcasted_iota(jnp.int32, (CHUNK, CHUNK), 0)
     qi = lax.broadcasted_iota(jnp.int32, (CHUNK, CHUNK), 1)
@@ -445,16 +458,16 @@
             rows = pl.ds(pl.multiple_of(h * HD, 8), HD)
             first, second = query_operands(kt[rows, 0:128], kt[rows, 128:256], gains[2])
             kd = key_operand(kt[rows, 256:384], kt[rows, 384:512], gains[3])
-            ve, vg = value_operands(kt[rows, 512:640], kt[rows, 640:768])
+            ve = value_operands(kt[rows, 512:640], kt[rows, 640:768])[0]
             both = dot(kd, jnp.concatenate([first, second], 1), ((1,), (0,)))
             s = jnp.where(place, both[:, 0:128], -1e30)
             e = jnp.exp2(s - jnp.max(s, 0, keepdims=True))
             g = e * both[:, 128:256]
-            of_e = dot(ve, e.astype(BF16), ((1,), (0,)))
-            of_g = dot(vg, g.astype(BF16), ((1,), (0,)))
+            sums = dot(ve, jnp.concatenate([e, g], 1).astype(BF16), ((1,), (0,)))
+            of_e, of_g = sums[:, 0:128], sums[:, 128:256]
             inv = 1.0 / of_e[144:145]
             attn = of_e[0:72] * inv
-            dattn = (of_e[72:144] + of_g[0:72] - of_g[73:74] * attn) * inv
+            dattn = (of_e[72:144] + of_g[0:72] - of_g[144:145] * attn) * inv
             to_rows = pl.ds(pl.multiple_of(lax.rem(h, 8) * HD, 8), HD)
             at[0, h // 8, to_rows, 0:128] = attn
             at[0, h // 8, to_rows, 128:256] = dattn
@@ -480,10 +493,6 @@
         for n in others:
             give_back(q, n).wait()
             forward(q, n).wait_send()
-        rows = pl.ds(pl.multiple_of(CHUNK * q, CHUNK), CHUNK)
-        z, dz = both_halves(got[q].astype(F32))
-        out_ref[0, rows, :] = z.astype(BF16)
-        out_ref[1, rows, :] = dz.astype(BF16)
         return 0
 
     lax.fori_loop(0, 2, collect, 0)
@@ -498,8 +507,10 @@
 
 
 def split_kernel(both_ref, out_ref, dout_ref):
-    out_ref[...] = both_ref[0]
-    dout_ref[...] = both_ref[1]
+    for q in range(2):
+        z, dz = both_halves(both_ref[q].astype(F32))
+        out_ref[CHUNK * q : CHUNK * (q + 1), :] = z.astype(BF16)
+        dout_ref[CHUNK * q : CHUNK * (q + 1), :] = dz.astype(BF16)
 
 
 def body(
@@ -524,7 +535,7 @@
     row = lambda gain: gain.reshape(1, HD)
     both = pl.pallas_call(
         block_kernel,
-        out_shape=jax.ShapeDtypeStruct((2, TOK, D), BF16),
+        out_shape=jax.ShapeDtypeStruct((2, 16, 16, D), BF16),
         in_specs=[vmem, vmem, vmem, vmem, hbm, hbm, vmem, vmem, hbm, hbm, vmem, vmem],
         out_specs=vmem,
         scratch_shapes=[
@@ -551,7 +562,6 @@
             pltpu.VMEM((2, 16, 16, D), BF16),
             pltpu.VMEM((2, 16, 16, D), BF16),
             pltpu.VMEM((2, 16, 16, D), BF16),
-            pltpu.VMEM((2, 16, 16, D), BF16),
             pltpu.VMEM((4, HD, 1), F32),
             pltpu.SemaphoreType.REGULAR((4,)),
             dma((2,)), dma((2,)), dma((5,)), dma((4,)), dma((2,)), dma((1,)), dma((11,)),

time: 116 us -> 109 us (0.940)
  Pallas kernels: 115 us -> 108 us
    pallas_call x1, Pallas kernels: 113 us -> 105 us  [body(): pl.pallas_call(block_kernel, out_shape=jax.ShapeDtypeStruct((2, 16, 16, D...]
where the time goes in v2:
time: 109 us; the launch traced here: 108 us
  Pallas kernels  108 us (99%)
    pallas_call x1, Pallas kernels, body(): pl.pallas_call(block_kernel, out_shape=jax.ShapeDtypeStruct((2, 16, 16, D...  105 us
    pallas_call x1, Pallas kernels, body(): pl.pallas_call(split_kernel, out_shape=(one, one), in_specs=[vmem], out_s...  2.34 us

profile of v2, /device:TPU:1, one launch (start us, length us, event | category | flops | bytes accessed | tf_op | source)
XLA Modules:
  0.0 108.3 jit_solution(1937092423176952489)
XLA Ops:
  0.6 105.3 %blocks.1.both_ref = bf16[2,16,16,1152]{3,2,1,0:T(8,128)(2,1)} custom-call(bf16[256,1152]{1,0:T(8,128)(2,1)} %bitcast.8, bf16[256,1152]{1,0:T(8,128)(2,1)} %bitcast.9, f32[3,1152]{1,0:T(4,128)} %mod_ref.1, f32[3,1152]{1,0:T(4,128)} %dmod_ref.1, bf16[1152,3456]{1,0:T(8,128)(2,1)} %wqkv_s.1, bf16[1152,1152]{1,0:T(8,128)(2,1)} %wout_s.1, f32[1,72]{1,0:T(1,128)} %bitcast.12, ...), custom_call_target="tpu_custom_call" | custom-call | flops 52999999488 | bytes 25000000 | tf_op jit(solution)/shard_map/blocks/pallas_call | solution.py:536
  105.9 2.3 %results.1 = (bf16[256,1152]{1,0:T(8,128)(2,1)}, bf16[256,1152]{1,0:T(8,128)(2,1)}) custom-call(bf16[2,16,16,1152]{3,2,1,0:T(8,128)(2,1)} %blocks.1.both_ref), custom_call_target="tpu_custom_call" | custom-call | tf_op jit(solution)/shard_map/results/pallas_call | solution.py:580

commit v3 on v2

--- a/solution.py
+++ b/solution.py
@@ -48,7 +48,7 @@
         put(at, rows, hidden.astype(BF16), dhidden.astype(BF16))
         return 0
 
-    lax.fori_loop(0, count // rows, step, 0)
+    lax.fori_loop(0, count // rows, step, 0, unroll=2)
 
 
 def head_norm(u, du):
@@ -111,11 +111,11 @@
 
 
 def block_kernel(
-    z_ref, dz_ref, mod_ref, dmod_ref, wqkv_s, wout_s, qg_s, kg_s, wqkv_t, wout_t, qg_t, kg_t,
+    z_hbm, dz_hbm, mod_ref, dmod_ref, wqkv_s, wout_s, qg_s, kg_s, wqkv_t, wout_t, qg_t, kg_t,
     got,
-    hb, zb, stage, wtmp, wt, wos, wtt, wot, kt, qs, qd, kds, ves, vgs, acc, mx, at, mine, theirs,
+    zin, hb, zb, stage, wtmp, wt, wos, wtt, wot, kt, qs, qd, kds, ves, vgs, acc, mx, at, mine, theirs,
     th, tx, rx, ty, gains,
-    relay, stage_sem, wsem, ro, rb, rz, rx_sem, ss, sw_s, sw_r, fs, fr, fl, gs, gr, gl,
+    relay, zin_sem, stage_sem, wsem, ro, rb, rz, tr_s, tr_r, ss, sw_s, sw_r, fs, fr, fl, gs, gr, gl,
 ):
     zh, y, c, zl, x = coords()
     right = (zh, y, c, zl, lax.rem(x + 1, 4))
@@ -126,6 +126,13 @@
     me = member(zh, y, zl)
     same = t == 0
     moved = t == 1
+
+    z_ref, dz_ref = zin.at[0], zin.at[1]
+    zin_copies = [
+        pltpu.make_async_copy(ref, zin.at[n], zin_sem.at[n]) for n, ref in enumerate((z_hbm, dz_hbm))
+    ]
+    for copy in zin_copies:
+        copy.start()
 
     barrier = pltpu.get_barrier_semaphore()
 
@@ -186,6 +193,8 @@
     swap_dz = remote(dz_ref, zb.at[1], ss.at[9], rz.at[1], partner)
 
     own = 8 * t
+    for copy in zin_copies:
+        copy.wait()
     for q in range(4):
 
         def put(at_row, rows, h, dh):
@@ -257,8 +266,10 @@
         def make_query(h, _):
             rows = pl.ds(pl.multiple_of(h * HD, 8), HD)
             first, second = query_operands(kt[rows, 0:256], kt[rows, 256:512], gains[0])
-            qs[h, :, 256 * part : 256 * part + 256] = first
-            qd[h, :, 256 * part : 256 * part + 256] = second
+            for q in range(2):
+                to = slice(256 * q + 128 * part, 256 * q + 128 * part + 128)
+                qs[h, :, to] = first[:, 128 * q : 128 * q + 128]
+                qd[h, :, to] = second[:, 128 * q : 128 * q + 128]
             return 0
 
         lax.fori_loop(0, HALF, make_query, 0, unroll=4)
@@ -290,6 +301,44 @@
     hear(2)
     pl.semaphore_signal(relay.at[3], inc=1, device_id=sib, device_id_type=MESH)
 
+    def keys_of(index, s):
+        kt[:, 512 * s : 512 * s + 512] = dot(wt[576:1728, :], hb[index].reshape(2 * TOK, D), ((1,), (1,)))
+
+    def prepare(h):
+        krow = pl.ds(pl.multiple_of(h * HD, 8), HD)
+        vrow = pl.ds(pl.multiple_of(576 + h * HD, 8), HD)
+        for s in range(2):
+            o = 512 * s
+            keys = slice(256 * s, 256 * s + 256)
+            kds[h, keys, :] = key_operand(kt[krow, o : o + 256], kt[krow, o + 256 : o + 512], gains[1])
+            ve, vg = value_operands(kt[vrow, o : o + 256], kt[vrow, o + 256 : o + 512])
+            ves[h, :, keys] = ve
+            vgs[h, :, keys] = vg
+
+    def attend(h, cols):
+        kd = kds[h]
+        s = dot(kd, qs[h, :, cols], ((1,), (0,)))
+        ds = dot(kd, qd[h, :, cols], ((1,), (0,)))
+        old = mx[h, 0:1, cols]
+        new = jnp.maximum(old, jnp.max(s, 0, keepdims=True))
+        mx[h, 0:1, cols] = new
+        e = jnp.exp2(s - new)
+        g = e * ds
+        keep = jnp.exp2(old - new)
+        of_e = dot(ves[h], e.astype(BF16), ((1,), (0,)))
+        of_g = dot(vgs[h], g.astype(BF16), ((1,), (0,)))
+        acc[h, 0:72, cols] = acc[h, 0:72, cols] * keep + of_e[0:72]
+        acc[h, 72:152, cols] = acc[h, 72:152, cols] * keep + of_e[72:152] + of_g
+
+    def heads(start, stop, cols, with_keys):
+        def one_head(h, _):
+            if with_keys:
+                prepare(h)
+            attend(h, cols)
+            return 0
+
+        lax.fori_loop(start, stop, one_head, 0, unroll=stop - start)
+
     def two_shards(i, _):
         @pl.when((i == 1) & moved)
         def _():
@@ -313,83 +362,42 @@
             to_sib[1].wait_recv()
             to_sib[3].wait_recv()
 
-        @pl.when((i == 3) & moved)
-        def _():
-            on_left.wait_recv()
-            on_right.wait_recv()
-            to_sib[2].start()
-
-        @pl.when(i == 3)
-        def _():
-            to_sib[2].wait_recv()
-
-        first = jnp.where(i == 0, 0, i + 1)
-        second = jnp.where(i == 0, 1, jnp.where(i == 3, 5, i + 5))
-        for s, index in enumerate((first, second)):
-            kt[:, 512 * s : 512 * s + 512] = dot(wt[576:1728, :], hb[index].reshape(2 * TOK, D), ((1,), (1,)))
-
-        def one_head(h, _):
-            krow = pl.ds(pl.multiple_of(h * HD, 8), HD)
-            vrow = pl.ds(pl.multiple_of(576 + h * HD, 8), HD)
-            for s in range(2):
-                o = 512 * s
-                keys = slice(256 * s, 256 * s + 256)
-                kds[h, keys, :] = key_operand(kt[krow, o : o + 256], kt[krow, o + 256 : o + 512], gains[1])
-                ve, vg = value_operands(kt[vrow, o : o + 256], kt[vrow, o + 256 : o + 512])
-                ves[h, :, keys] = ve
-                vgs[h, :, keys] = vg
-            kd = kds[h]
-            s = dot(kd, qs[h], ((1,), (0,)))
-            ds = dot(kd, qd[h], ((1,), (0,)))
-            old = mx[h, 0:1, :]
-            new = jnp.maximum(old, jnp.max(s, 0, keepdims=True))
-            mx[h, 0:1, :] = new
-            e = jnp.exp2(s - new)
-            g = e * ds
-            keep = jnp.exp2(old - new)
-            of_e = dot(ves[h], e.astype(BF16), ((1,), (0,)))
-            of_g = dot(vgs[h], g.astype(BF16), ((1,), (0,)))
-            acc[h, 0:72, :] = acc[h, 0:72, :] * keep + of_e[0:72]
-            acc[h, 72:152, :] = acc[h, 72:152, :] * keep + of_e[72:152] + of_g
+        keys_of(jnp.where(i == 0, 0, i + 1), 0)
+        keys_of(jnp.where(i == 0, 1, i + 5), 1)
+        heads(0, HALF, slice(0, 512), True)
+        return 0
+
+    lax.fori_loop(0, 3, two_shards, 0)
+
+    @pl.when(moved)
+    def _():
+        on_left.wait_recv()
+        on_right.wait_recv()
+        to_sib[2].start()
+
+    to_sib[2].wait_recv()
+    keys_of(4, 0)
+    keys_of(5, 1)
+    heads(0, HALF, slice(0, 256), True)
+
+    trades = [remote(mine.at[1, q], theirs.at[q], tr_s.at[q], tr_r.at[q], sib) for q in range(2)]
+
+    def finish(q):
+        def finish_head(h, _):
+            attn, dattn = normalised(acc[h, :, 256 * q : 256 * q + 256])
+            rows = pl.ds(pl.multiple_of(h * HD, 8), HD)
+            for part in range(2):
+                at[part, q, rows, 0:128] = attn[:, 128 * part : 128 * part + 128]
+                at[part, q, rows, 128:256] = dattn[:, 128 * part : 128 * part + 128]
             return 0
 
-        lax.fori_loop(0, HALF, one_head, 0, unroll=8)
-        return 0
-
-    lax.fori_loop(0, 4, two_shards, 0)
-
-    def finish_head(h, _):
-        attn, dattn = normalised(acc[h])
-        rows = pl.ds(pl.multiple_of(h * HD, 8), HD)
-        for part in range(2):
-            for q in range(2):
-                cols = slice(256 * part + 128 * q, 256 * part + 128 * q + 128)
-                at[part, q, rows, 0:128] = attn[:, cols]
-                at[part, q, rows, 128:256] = dattn[:, cols]
-        return 0
-
-    lax.fori_loop(0, HALF, finish_head, 0, unroll=2)
-    mine[1] = at[1 - t].astype(BF16)
-    trade = remote(mine.at[1], theirs, ss.at[10], rx_sem.at[0], sib)
-    trade.start()
-    mine[0] = at[t].astype(BF16)
-    out_w[0].wait()
-    out_w[1].wait()
+        lax.fori_loop(0, HALF, finish_head, 0, unroll=4)
+        mine[1, q] = at[1 - t, q].astype(BF16)
+        trades[q].start()
+        mine[0, q] = at[t, q].astype(BF16)
+
     lo = pl.ds(pl.multiple_of(576 * c, 16), 576)
     hi = pl.ds(pl.multiple_of(576 * (1 - c), 16), 576)
-
-    def own_heads(q):
-        return dot(mine[0, q], wos[lo, :], ((0,), (0,)))
-
-    own_part = own_heads(0)
-
-    @pl.when(moved)
-    def _():
-        swap_z.wait_recv()
-        swap_dz.wait_recv()
-
-    trade.wait_recv()
-    pl.semaphore_wait(relay.at[3], 1)
 
     def forward(q, n):
         a, b, d = OFFSETS[n]
@@ -415,8 +423,10 @@
     gate = mod_ref[2:3, :]
     dgate = dmod_ref[2:3, :]
 
-    def spatial_out(q, part):
-        both = part + dot(theirs[q], wos[hi, :], ((0,), (0,)))
+    def spatial_out(q):
+        both = dot(mine[0, q], wos[lo, :], ((0,), (0,)))
+        trades[q].wait_recv()
+        both += dot(theirs[q], wos[hi, :], ((0,), (0,)))
         rows = pl.ds(CHUNK * q, CHUNK)
         proj, dproj = both[0:CHUNK], both[CHUNK:]
         tx[q] = joined(
@@ -429,9 +439,25 @@
         for n in others:
             forward(q, n).start()
 
-    spatial_out(0, own_part)
+    finish(0)
+    heads(0, 4, slice(256, 512), False)
+    out_w[0].wait()
+    out_w[1].wait()
+
+    @pl.when(moved)
+    def _():
+        swap_z.wait_recv()
+        swap_dz.wait_recv()
+
+    pl.semaphore_wait(relay.at[3], 1)
+    spatial_out(0)
     send(0)
-    spatial_out(1, own_heads(1))
+    heads(4, HALF, slice(256, 512), False)
+    finish(1)
+    spatial_out(1)
+    for n in others:
+        forward(0, n).wait_send()
+    send(1)
 
     ki = lax.broadcasted_iota(jnp.int32, (CHUNK, CHUNK), 0)
     qi = lax.broadcasted_iota(jnp.int32, (CHUNK, CHUNK), 1)
@@ -441,7 +467,6 @@
         forward_own(q).wait()
         for n in others:
             forward(q, n).wait_recv()
-        pl.when(q == 0)(lambda: send(1))
 
         def put(at_row, rows, h, dh):
             th[pl.ds(at_row, rows), :] = h
@@ -492,12 +517,13 @@
         pl.when(moved)(lambda: give_back(q, SELF).wait())
         for n in others:
             give_back(q, n).wait()
-            forward(q, n).wait_send()
         return 0
 
     lax.fori_loop(0, 2, collect, 0)
 
-    for copy in (to_right, to_left, *to_sib, on_left, on_right, trade):
+    for n in others:
+        forward(1, n).wait_send()
+    for copy in (to_right, to_left, *to_sib, on_left, on_right, *trades):
         copy.wait_send()
 
     @pl.when(moved)
@@ -536,9 +562,10 @@
     both = pl.pallas_call(
         block_kernel,
         out_shape=jax.ShapeDtypeStruct((2, 16, 16, D), BF16),
-        in_specs=[vmem, vmem, vmem, vmem, hbm, hbm, vmem, vmem, hbm, hbm, vmem, vmem],
+        in_specs=[hbm, hbm, vmem, vmem, hbm, hbm, vmem, vmem, hbm, hbm, vmem, vmem],
         out_specs=vmem,
         scratch_shapes=[
+            pltpu.VMEM((2, TOK, D), BF16),
             pltpu.VMEM((9, 2, TOK, D), BF16),
             pltpu.VMEM((2, TOK, D), BF16),
             pltpu.VMEM((2, D, 640), BF16),
@@ -564,7 +591,7 @@
             pltpu.VMEM((2, 16, 16, D), BF16),
             pltpu.VMEM((4, HD, 1), F32),
             pltpu.SemaphoreType.REGULAR((4,)),
-            dma((2,)), dma((2,)), dma((5,)), dma((4,)), dma((2,)), dma((1,)), dma((11,)),
+            dma((2,)), dma((2,)), dma((2,)), dma((5,)), dma((4,)), dma((2,)), dma((2,)), dma((2,)), dma((10,)),
             dma((4,)), dma((4,)),
             dma((32,)), dma((32,)), dma((2,)), dma((32,)), dma((32,)), dma((2,)),
         ],

time: 109 us -> 105 us (0.963)
  Pallas kernels: 108 us -> 104 us
    pallas_call x1, Pallas kernels: 105 us -> 102 us  [body(): pl.pallas_call(block_kernel, out_shape=jax.ShapeDtypeStruct((2, 16, 16, D...]
where the time goes in v3:
time: 105 us
  Pallas kernels  104 us (99%)
    pallas_call x1, Pallas kernels, body(): pl.pallas_call(block_kernel, out_shape=jax.ShapeDtypeStruct((2, 16, 16, D...  102 us
    pallas_call x1, Pallas kernels, body(): pl.pallas_call(split_kernel, out_shape=(one, one), in_specs=[vmem], out_s...  2.34 us

profile of v3, /device:TPU:1, one launch (start us, length us, event | category | flops | bytes accessed | tf_op | source)
XLA Modules:
  0.0 105.0 jit_solution(15565383438375042411)
XLA Ops:
  0.6 102.0 %blocks.1.both_ref = bf16[2,16,16,1152]{3,2,1,0:T(8,128)(2,1)} custom-call(bf16[256,1152]{1,0:T(8,128)(2,1)} %bitcast.8, bf16[256,1152]{1,0:T(8,128)(2,1)} %bitcast.9, f32[3,1152]{1,0:T(4,128)} %mod_ref.1, f32[3,1152]{1,0:T(4,128)} %dmod_ref.1, bf16[1152,3456]{1,0:T(8,128)(2,1)} %wqkv_s.1, bf16[1152,1152]{1,0:T(8,128)(2,1)} %wout_s.1, f32[1,72]{1,0:T(1,128)} %bitcast.12, ...), custom_call_target="tpu_custom_call" | custom-call | flops 52999999488 | bytes 25000000 | tf_op jit(solution)/shard_map/blocks/pallas_call | solution.py:562
  102.7 2.3 %results.1 = (bf16[256,1152]{1,0:T(8,128)(2,1)}, bf16[256,1152]{1,0:T(8,128)(2,1)}) custom-call(bf16[2,16,16,1152]{3,2,1,0:T(8,128)(2,1)} %blocks.1.both_ref), custom_call_target="tpu_custom_call" | custom-call | tf_op jit(solution)/shard_map/results/pallas_call | solution.py:607

commit v4 on v3

--- a/solution.py
+++ b/solution.py
@@ -290,10 +290,8 @@
     @pl.when(same)
     def _():
         to_left.wait_recv()
-        on_left.start()
         to_sib[1].start()
         to_right.wait_recv()
-        on_right.start()
         to_sib[3].start()
         to_sib[0].wait_recv()
 
@@ -340,6 +338,11 @@
         lax.fori_loop(start, stop, one_head, 0, unroll=stop - start)
 
     def two_shards(i, _):
+        @pl.when((i == 1) & same)
+        def _():
+            on_left.start()
+            on_right.start()
+
         @pl.when((i == 1) & moved)
         def _():
             to_sib[1].wait_recv()

time: 105 us -> 104 us (level)
    pallas_call x1, Pallas kernels: 102 us -> 100 us  [body(): pl.pallas_call(block_kernel, out_shape=jax.ShapeDtypeStruct((2, 16, 16, D...]
where the time goes in v4:
time: 104 us; the launch traced here: 103 us
  Pallas kernels  103 us (99%)
    pallas_call x1, Pallas kernels, body(): pl.pallas_call(block_kernel, out_shape=jax.ShapeDtypeStruct((2, 16, 16, D...  100 us
    pallas_call x1, Pallas kernels, body(): pl.pallas_call(split_kernel, out_shape=(one, one), in_specs=[vmem], out_s...  2.34 us

profile of v4, /device:TPU:1, one launch (start us, length us, event | category | flops | bytes accessed | tf_op | source)
XLA Modules:
  0.0 103.2 jit_solution(14786324204636935204)
XLA Ops:
  0.6 100.2 %blocks.1.both_ref = bf16[2,16,16,1152]{3,2,1,0:T(8,128)(2,1)} custom-call(bf16[256,1152]{1,0:T(8,128)(2,1)} %bitcast.8, bf16[256,1152]{1,0:T(8,128)(2,1)} %bitcast.9, f32[3,1152]{1,0:T(4,128)} %mod_ref.1, f32[3,1152]{1,0:T(4,128)} %dmod_ref.1, bf16[1152,3456]{1,0:T(8,128)(2,1)} %wqkv_s.1, bf16[1152,1152]{1,0:T(8,128)(2,1)} %wout_s.1, f32[1,72]{1,0:T(1,128)} %bitcast.12, ...), custom_call_target="tpu_custom_call" | custom-call | flops 52999999488 | bytes 25000000 | tf_op jit(solution)/shard_map/blocks/pallas_call | solution.py:565
  100.8 2.3 %results.1 = (bf16[256,1152]{1,0:T(8,128)(2,1)}, bf16[256,1152]{1,0:T(8,128)(2,1)}) custom-call(bf16[2,16,16,1152]{3,2,1,0:T(8,128)(2,1)} %blocks.1.both_ref), custom_call_target="tpu_custom_call" | custom-call | tf_op jit(solution)/shard_map/results/pallas_call | solution.py:610
